TPU v7x, 256 devices: a whole 4x4x8 slice. The times are simulated.
256 devices in a mesh: tm: 32 (over z, y), dp: 8 (over x, core).
Axes of the slice: x: 4, y: 4, z: 8, core: 2. Of those that a mesh axis runs over, the one named last changes fastest.
Arguments:
- inputs: bfloat16 [8, 32768, 1024], P('dp', 'tm'), may hold values from -6 to 6
- weights: bfloat16 [1024, 1536], replicated, may hold values from -0.1875 to 0.1875
- out_grad: bfloat16 [8, 32768, 512], P('dp', 'tm'), may hold values from -6 to 6
Outputs:
- input_grad: bfloat16 [8, 32768, 1024], P('dp', 'tm')
- weight_grad: float32 [1024, 1536], P('tm')
All inputs are finite; a program needn't handle non-finite values.
Results may differ from a plain program's by a relative error of at most 0.0075.
Values sent between devices are 32-bit elements; how exact they have to be, the bound alone decides.
No kernel may reach another device: no remote copies, remote signals or barrier semaphores. Data moves between devices by JAX's collectives and lax.ppermute only.
A program may use at most 128 MiB of HBM per device.

v0:
```python
import jax
import jax.numpy as jnp
from jax import lax
from jax.sharding import PartitionSpec as P

H = 4
HD = 128
CH = 256


def carried_in(value, axis, join, neutral, backward):
    count, mine = (lax.axis_size(axis), lax.axis_index(axis))
    pieces = lax.all_gather(value, axis)
    if backward:
        pieces = pieces[::-1]
        mine = count - 1 - mine
    so_far = jnp.full_like(value, 0) + jnp.asarray(neutral, value.dtype)

    def lap(position, so_far):
        longer = join(so_far, pieces[position])
        return jnp.where(position < mine, longer, so_far)

    return lax.fori_loop(0, count - 1, lap, so_far)


def combine(earlier, later):
    return jax.tree.map(jnp.add, earlier, later)


def shards(inputs, weights, out_grad):
    f32 = jnp.float32
    bf16 = jnp.bfloat16
    tok_count = inputs.shape[1]
    width = weights.shape[1] // 3
    block_count = tok_count // CH
    record = inputs[0]
    qkv = jnp.dot(record, weights, preferred_element_type=f32).astype(bf16)
    shape4 = (block_count, CH, H, HD)
    queries = qkv[:, :width].reshape(shape4)
    key_rows = qkv[:, width : 2 * width].reshape(shape4)
    values = qkv[:, 2 * width :].reshape(shape4)
    offset = lax.axis_index("tm") * tok_count
    position = (offset + jnp.arange(tok_count, dtype=jnp.int32)).astype(f32)
    factor = 1.0 / jnp.sqrt(jnp.float32(HD) * (position + 1.0))
    scaled_grad = (out_grad[0].astype(f32) * factor[:, None]).astype(bf16).reshape(shape4)
    tri = (
        lax.broadcasted_iota(jnp.int32, (CH, CH), 0) >= lax.broadcasted_iota(jnp.int32, (CH, CH), 1)
    ).astype(f32)
    kv_group = jnp.einsum("nshd,nshe->nhde", key_rows, values, preferred_element_type=f32)
    qg_group = jnp.einsum("nthd,nthe->nhde", queries, scaled_grad, preferred_element_type=f32)
    kv_device = jnp.sum(kv_group, 0)
    qg_device = jnp.sum(qg_group, 0)
    zeros = jnp.zeros((H, HD, HD), f32)
    state_start = carried_in(kv_device, "tm", combine, zeros, False)
    grad_end = carried_in(qg_device, "tm", combine, zeros, True)
    mix_vg = (
        jnp.einsum("nthe,nshe->nhts", scaled_grad, values, preferred_element_type=f32) * tri
    ).astype(bf16)
    mix_qk = (
        jnp.einsum("nthd,nshd->nhts", queries, key_rows, preferred_element_type=f32) * tri
    ).astype(bf16)
    state_before = (state_start[None] + jnp.cumsum(kv_group, 0) - kv_group).astype(bf16)
    grad_after = (
        grad_end[None] + jnp.flip(jnp.cumsum(jnp.flip(qg_group, 0), 0), 0) - qg_group
    ).astype(bf16)
    grad_q = jnp.einsum(
        "nhts,nshd->nthd", mix_vg, key_rows, preferred_element_type=f32
    ) + jnp.einsum("nthe,nhde->nthd", scaled_grad, state_before, preferred_element_type=f32)
    grad_k = jnp.einsum(
        "nhts,nthd->nshd", mix_vg, queries, preferred_element_type=f32
    ) + jnp.einsum("nshe,nhde->nshd", values, grad_after, preferred_element_type=f32)
    grad_v = jnp.einsum(
        "nhts,nthe->nshe", mix_qk, scaled_grad, preferred_element_type=f32
    ) + jnp.einsum("nshd,nhde->nshe", key_rows, grad_after, preferred_element_type=f32)
    dqkv = jnp.concatenate(
        [
            grad_q.reshape(tok_count, width),
            grad_k.reshape(tok_count, width),
            grad_v.reshape(tok_count, width),
        ],
        axis=1,
    ).astype(bf16)
    record_grad = lax.dot_general(
        dqkv, weights, (((1,), (1,)), ((), ())), preferred_element_type=f32
    ).astype(bf16)
    partial_rows = lax.psum_scatter(
        lax.dot_general(record, dqkv, (((0,), (0,)), ((), ())), preferred_element_type=f32),
        "tm",
        scatter_dimension=0,
        tiled=True,
    )
    proj_grad = lax.psum(partial_rows, "dp")
    return (record_grad[None], proj_grad)


def solution(mesh):
    placed = (P("dp", "tm", None), P(), P("dp", "tm", None))
    return jax.shard_map(
        shards,
        mesh=mesh,
        in_specs=placed,
        out_specs=(P("dp", "tm", None), P("tm", None)),
        check_vma=False,
    )
```

profile of v0, /device:TPU:8, one launch (start us, length us, event | category | flops | bytes accessed | tf_op | source)
XLA Modules:
  0.0 592.0 jit_solution(9342990960004668326)
XLA Ops:
  7.2 2.8 reshape.58
  10.1 2.9 copy.36
  13.0 5.2 convolution_convert_fusion
  20.0 2.2 reshape.55
  22.1 1.9 multiply_convert_fusion.2
  25.1 2.2 fusion.27
  27.4 2.2 reshape.53
  29.5 2.1 reshape.52
  31.7 3.8 fusion.26
  35.7 2.3 rev.11
  38.0 2.5 fusion.28
  40.5 2.3 multiply_convert_fusion.1
  42.9 1.9 fusion.10
  44.7 2.2 fusion.19
  46.9 4.3 fusion.2
  51.1 76.5 %all-gather.7.cloned.1.call-done = f32[128,128,128]{2,1,0:T(8,128)} async-done(((f32[4,128,128]{2,1,0:T(8,128)}), f32[128,128,128]{2,1,0:T(8,128)}) %all-gather.7.cloned.1.call-update) | async-done | bytes 8388624 | tf_op jit(solution)/shard_map/all_gather | solution.py:13
  127.6 7.7 %rev.10 = f32[32,4,128,128]{3,2,1,0:T(8,128)} reverse(f32[32,4,128,128]{3,2,1,0:T(8,128)} %bitcast.53), dimensions={0} | reverse | bytes 16777216 | tf_op jit(solution)/shard_map/rev | solution.py:15
  135.4 54.8 %while.29 = (s32[]{:T(128)}, f32[4,128,128]{2,1,0:T(8,128)}, s32[]{:T(128)}, f32[32,4,128,128]{3,2,1,0:T(8,128)}, s32[]{:T(128)}, /*index=5*/s32[]{:T(128)}) while((s32[]{:T(128)}, f32[4,128,128]{2,1,0:T(8,128)}, s32[]{:T(128)}, f32[32,4,128,128]{3,2,1,0:T(8,128)}, s32[]{:T(128)}, /*index=5*/s32[]{:T(128)}) %tuple.73), condition=%wide.region_6.7_spmd.clone, body=%wide.region_5.6_spmd.clone.sunk | while | flops 196612 | bytes 786525 | solution.py:23
  140.6 1.8 add_select_fusion.5
  144.1 1.8 add_select_fusion.5
  147.7 1.8 add_select_fusion.5
  151.2 1.8 add_select_fusion.5
  154.7 1.8 add_select_fusion.5
  158.3 1.8 add_select_fusion.5
  165.4 1.8 add_select_fusion.5
  179.5 1.8 add_select_fusion.5
  186.6 1.8 add_select_fusion.5
  188.4 1.8 add_select_fusion.5
  190.2 1.9 subtract_convert_fusion
  192.9 3.2 fusion.5
  196.1 2.3 copy.48
  198.5 27.4 %all-gather.5.cloned.1.call-done = f32[128,128,128]{2,1,0:T(8,128)} async-done(((f32[4,128,128]{2,1,0:T(8,128)}), f32[128,128,128]{2,1,0:T(8,128)}) %all-gather.5.cloned.1.call-update) | async-done | bytes 8388624 | tf_op jit(solution)/shard_map/all_gather | solution.py:13
  225.9 33.0 %while.28 = (s32[]{:T(128)}, f32[4,128,128]{2,1,0:T(8,128)S(1)}, s32[]{:T(128)}, f32[32,4,128,128]{3,2,1,0:T(8,128)}, s32[]{:T(128)}, /*index=5*/s32[]{:T(128)}) while((s32[]{:T(128)}, f32[4,128,128]{2,1,0:T(8,128)S(1)}, s32[]{:T(128)}, f32[32,4,128,128]{3,2,1,0:T(8,128)}, s32[]{:T(128)}, /*index=5*/s32[]{:T(128)}) %tuple.84), condition=%wide.region_2.3_spmd.clone, body=%wide.region_1.0_spmd.clone.sunk | while | flops 196612 | bytes 786525 | solution.py:23
  258.9 1.8 fusion.7
  260.7 3.0 fusion.4
  263.8 2.3 copy.43
  266.1 2.5 bitcast_dynamic-update-slice_fusion.2
  268.6 2.9 fusion.6
  271.5 2.4 copy.53
  273.9 2.6 bitcast_dynamic-update-slice_fusion.1
  276.5 2.4 bitcast_dynamic-update-slice_fusion
  278.9 7.3 %convolution_bitcast_fusion = f32[1024,1536]{0,1:T(8,128)} fusion(bf16[1024,1536]{1,0:T(8,128)(2,1)} %bitcast_dynamic-update-slice_fusion, bf16[1,1024,1024]{2,1,0:T(8,128)(2,1)S(1)} %copy-done.10), kind=kOutput, calls=%fused_computation.2 | convolution fusion | flops 3221225472 | bytes 11534336 | tf_op jit(solution)/shard_map/dot_general | solution.py:87
  286.2 6.6 %copy.59 = f32[1024,1536]{1,0:T(8,128)} copy(f32[1024,1536]{0,1:T(8,128)} %convolution_bitcast_fusion) | data formatting | bytes 12582912
  292.9 222.4 %reduce-scatter.4.cloned.1.call-done = f32[32,1536]{1,0:T(8,128)} async-done(((f32[1024,1536]{1,0:T(8,128)}), f32[32,1536]{1,0:T(8,128)}) %reduce-scatter.4.cloned.1.call-update) | async-done | bytes 196624
  515.3 2.1 copy.60
  517.4 6.5 %convert_bitcast_fusion = bf16[1,1024,1024]{2,1,0:T(8,128)(2,1)} fusion(bf16[1024,1536]{1,0:T(8,128)(2,1)} %bitcast_dynamic-update-slice_fusion, bf16[1024,1536]{1,0:T(8,128)(2,1)S(1)} %copy-done), kind=kOutput, calls=%fused_computation.8 | convolution fusion | flops 3222274048 | bytes 8388608 | tf_op jit(solution)/shard_map/dot_general | solution.py:83
  523.9 59.5 %all-reduce.2.cloned.1.call-done = f32[32,1536]{0,1:T(8,128)} async-done(((f32[32,1536]{0,1:T(8,128)}), f32[32,1536]{0,1:T(8,128)}) %all-reduce.2.cloned.1.call-update) | async-done | bytes 196624 | tf_op jit(solution)/shard_map/psum | solution.py:92
  583.4 2.1 copy.54
  (87 shorter events, 73.4 us)
Async XLA Ops:
  7.2 5.9 copy-start
  7.2 120.5 %all-gather.7.cloned.1.call-start = ((), (), s32[]{:S(2)}) async-start(), calls=%async_computation.3 | async-start | bytes 8650752 | tf_op jit(solution)/shard_map/all_gather | solution.py:13
  22.1 3.0 copy-start.5
  24.0 1.1 copy-start.1
  27.3 198.6 %all-gather.5.cloned.1.call-start = ((), (), s32[]{:S(2)}) async-start(), calls=%async_computation.2 | async-start | bytes 8650752 | tf_op jit(solution)/shard_map/all_gather | solution.py:13
  35.5 479.8 %reduce-scatter.4.cloned.1.call-start = ((), (), s32[]{:S(2)}) async-start(), calls=%async_computation.4 | async-start | bytes 6488064
  38.0 4.8 copy-start.9
  38.0 4.8 copy-start.6
  42.8 1.9 copy-start.3
  190.2 2.7 copy-start.4
  192.1 0.8 copy-start.8
  258.9 1.9 copy-start.2
  266.1 2.5 copy-start.7
  273.9 5.0 copy-start.10
  292.8 290.6 %all-reduce.2.cloned.1.call-start = ((), (), s32[]{:S(2)}) async-start(), calls=%async_computation.1 | async-start | bytes 1572864 | tf_op jit(solution)/shard_map/psum | solution.py:92
Sparse Core Ops, SparseCore 0:
  27.4 100.1 all-gather.6
  130.2 95.6 all-gather.4
  292.9 222.3 reduce-scatter.3
  517.6 65.7 all-reduce.1
where the time goes:
time: 594 us; the launch traced here: 592 us
  waiting for transfers between devices  386 us (65%)
  other arithmetic  95.1 us (16%)
  local copies, waits for them, and re-layouts  51.2 us (9%)
  matrix products  44.8 us (8%)
  between operations  13.9 us (2%)
    unnamed x5, waiting for transfers between devices  222 us
    all_gather x2, waiting for transfers between devices, carried_in(): pieces = lax.all_gather(value, axis)  104 us
    select_n x62, other arithmetic, lap(): return jnp.where(position < mine, longer, so_far)  87.1 us
    psum x1, waiting for transfers between devices, shards(): proj_grad = lax.psum(partial_rows, 'dp')  59.5 us
    unnamed x27, local copies, waits for them, and re-layouts  17.8 us
  transfers between devices with their start and end apart: 4, of which 4 were waited for; matrix products, arithmetic and copies ran while one was open for 17% of the time, Pallas kernels for 0%

commit v1 on v0

--- a/solution.py
+++ b/solution.py
@@ -89,7 +89,11 @@
         scatter_dimension=0,
         tiled=True,
     )
-    proj_grad = lax.psum(partial_rows, "dp")
+    proj_grad = partial_rows
+    for hop in (1, 2, 4):
+        proj_grad = proj_grad + lax.ppermute(
+            proj_grad, "dp", [(dev, dev ^ hop) for dev in range(8)]
+        )
     return (record_grad[None], proj_grad)
 
 

time: 594 us -> 545 us (0.918)
  waiting for transfers between devices: 386 us -> 333 us
    unnamed x5 -> x3, waiting for transfers between devices: 222 us -> 0.05 us
    reduce_scatter x0 -> x1, waiting for transfers between devices: none -> 222 us  [shards(): lax.psum_scatter(lax.dot_general(record, dqkv, (((0,), (0,)), ((), ())),...]
    psum x1 -> x0, waiting for transfers between devices: 59.5 us -> none  [shards(): proj_grad = lax.psum(partial_rows, 'dp')]
    ppermute x0 -> x3, waiting for transfers between devices: none -> 7.13 us  [shards(): lax.ppermute(proj_grad, 'dp', [(dev, dev ^ hop) for dev in range(8)])]
    unnamed x27 -> x25, local copies, waits for them, and re-layouts: 17.8 us -> 13.6 us
  transfers between devices with their start and end apart: 4 -> 6, of which waited for: 4 -> 5; matrix products, arithmetic and copies ran while one was open for 17% -> 19% of each run, Pallas kernels for 0% -> 0%
where the time goes in v1:
time: 545 us; the launch traced here: 541 us
  waiting for transfers between devices  333 us (61%)
  other arithmetic  97.2 us (18%)
  local copies, waits for them, and re-layouts  47 us (9%)
  matrix products  44.9 us (8%)
  between operations  13.9 us (3%)
    reduce_scatter x1, waiting for transfers between devices, shards(): lax.psum_scatter(lax.dot_general(record, dqkv, (((0,), (0,)), ((), ())),...  222 us
    all_gather x2, waiting for transfers between devices, carried_in(): pieces = lax.all_gather(value, axis)  103 us
    select_n x62, other arithmetic, lap(): return jnp.where(position < mine, longer, so_far)  87.5 us
    unnamed x25, local copies, waits for them, and re-layouts  13.6 us
  transfers between devices with their start and end apart: 6, of which 5 were waited for; matrix products, arithmetic and copies ran while one was open for 19% of the time, Pallas kernels for 0%

profile of v1, /device:TPU:8, one launch (start us, length us, event | category | flops | bytes accessed | tf_op | source)
XLA Modules:
  0.0 541.4 jit_solution(535146883355288134)
XLA Ops:
  7.2 2.8 reshape.58
  10.1 2.9 copy.61
  13.0 5.2 convolution_convert_fusion
  20.0 2.1 reshape.55
  22.1 1.9 multiply_convert_fusion.2
  25.1 2.2 fusion.27
  27.4 2.1 reshape.53
  29.5 2.1 reshape.52
  31.6 3.8 fusion.26
  35.7 2.3 rev.11
  38.0 2.4 fusion.28
  40.5 2.3 multiply_convert_fusion.1
  42.8 1.9 fusion.10
  44.7 2.2 fusion.19
  46.8 4.3 fusion.2
  51.1 76.5 %all-gather.7.cloned.1.call-done = f32[128,128,128]{2,1,0:T(8,128)} async-done(((f32[4,128,128]{2,1,0:T(8,128)}), f32[128,128,128]{2,1,0:T(8,128)}) %all-gather.7.cloned.1.call-update) | async-done | bytes 8388624 | tf_op jit(solution)/shard_map/all_gather | solution.py:13
  127.6 7.7 %rev.10 = f32[32,4,128,128]{3,2,1,0:T(8,128)} reverse(f32[32,4,128,128]{3,2,1,0:T(8,128)} %bitcast.53), dimensions={0} | reverse | bytes 16777216 | tf_op jit(solution)/shard_map/rev | solution.py:15
  135.3 55.3 %while.29 = (s32[]{:T(128)}, f32[4,128,128]{2,1,0:T(8,128)}, s32[]{:T(128)}, f32[32,4,128,128]{3,2,1,0:T(8,128)}, s32[]{:T(128)}, /*index=5*/s32[]{:T(128)}) while((s32[]{:T(128)}, f32[4,128,128]{2,1,0:T(8,128)}, s32[]{:T(128)}, f32[32,4,128,128]{3,2,1,0:T(8,128)}, s32[]{:T(128)}, /*index=5*/s32[]{:T(128)}) %tuple.73), condition=%wide.region_6.7_spmd.clone, body=%wide.region_5.6_spmd.clone.sunk | while | flops 196612 | bytes 786525 | solution.py:23
  138.8 1.8 add_select_fusion.5
  140.6 1.8 add_select_fusion.5
  154.9 1.8 add_select_fusion.5
  158.5 1.8 add_select_fusion.5
  162.0 1.8 add_select_fusion.5
  163.8 1.8 add_select_fusion.5
  165.6 1.8 add_select_fusion.5
  179.8 1.8 add_select_fusion.5
  185.2 1.8 add_select_fusion.5
  187.0 1.8 add_select_fusion.5
  188.8 1.8 add_select_fusion.5
  190.6 1.9 subtract_convert_fusion
  193.3 3.3 fusion.5
  196.6 2.4 copy.73
  199.0 26.9 %all-gather.5.cloned.1.call-done = f32[128,128,128]{2,1,0:T(8,128)} async-done(((f32[4,128,128]{2,1,0:T(8,128)}), f32[128,128,128]{2,1,0:T(8,128)}) %all-gather.5.cloned.1.call-update) | async-done | bytes 8388624 | tf_op jit(solution)/shard_map/all_gather | solution.py:13
  225.9 33.0 %while.28 = (s32[]{:T(128)}, f32[4,128,128]{2,1,0:T(8,128)S(1)}, s32[]{:T(128)}, f32[32,4,128,128]{3,2,1,0:T(8,128)}, s32[]{:T(128)}, /*index=5*/s32[]{:T(128)}) while((s32[]{:T(128)}, f32[4,128,128]{2,1,0:T(8,128)S(1)}, s32[]{:T(128)}, f32[32,4,128,128]{3,2,1,0:T(8,128)}, s32[]{:T(128)}, /*index=5*/s32[]{:T(128)}) %tuple.82), condition=%wide.region_2.3_spmd.clone, body=%wide.region_1.0_spmd.clone.sunk | while | flops 196612 | bytes 786525 | solution.py:23
  258.9 1.8 fusion.7
  260.7 3.0 fusion.4
  263.8 2.3 copy.68
  266.1 2.5 bitcast_dynamic-update-slice_fusion.2
  268.6 2.9 fusion.6
  271.5 2.4 copy.78
  273.9 2.6 bitcast_dynamic-update-slice_fusion.1
  276.4 2.4 bitcast_dynamic-update-slice_fusion
  278.9 7.3 %convolution_bitcast_fusion = f32[1024,1536]{0,1:T(8,128)} fusion(bf16[1024,1536]{1,0:T(8,128)(2,1)} %bitcast_dynamic-update-slice_fusion, bf16[1,1024,1024]{2,1,0:T(8,128)(2,1)S(1)} %copy-done.10), kind=kOutput, calls=%fused_computation.2 | convolution fusion | flops 3221225472 | bytes 11534336 | tf_op jit(solution)/shard_map/dot_general | solution.py:87
  286.2 6.6 %copy.85 = f32[1024,1536]{1,0:T(8,128)} copy(f32[1024,1536]{0,1:T(8,128)} %convolution_bitcast_fusion) | data formatting | bytes 12582912
  292.8 222.2 %reduce-scatter.4.cloned.1.call-done = f32[32,1536]{1,0:T(8,128)} async-done(((f32[1024,1536]{1,0:T(8,128)}), f32[32,1536]{1,0:T(8,128)}) %reduce-scatter.4.cloned.1.call-update) | async-done | bytes 196624 | tf_op jit(solution)/shard_map/reduce_scatter | solution.py:86
  519.1 5.5 %collective-permute-done.1 = f32[32,1536]{1,0:T(8,128)S(1)} collective-permute-done((f32[32,1536]{1,0:T(8,128)S(1)}, f32[32,1536]{1,0:T(8,128)S(1)}, u32[]{:S(2)}, u32[]{:S(2)}) %collective-permute-start.1) | collective-permute-done | bytes 196640 | tf_op jit(solution)/shard_map/ppermute | solution.py:94
  524.6 3.1 collective-permute-start.2
  527.7 6.5 %convert_bitcast_fusion = bf16[1,1024,1024]{2,1,0:T(8,128)(2,1)} fusion(bf16[1024,1536]{1,0:T(8,128)(2,1)} %bitcast_dynamic-update-slice_fusion, bf16[1024,1536]{1,0:T(8,128)(2,1)S(1)} %copy-done), kind=kOutput, calls=%fused_computation.8 | convolution fusion | flops 3222274048 | bytes 8388608 | tf_op jit(solution)/shard_map/dot_general | solution.py:83
  (91 shorter events, 76.7 us)
Async XLA Ops:
  7.2 5.8 %copy-start = (bf16[1024,1536]{1,0:T(8,128)(2,1)S(1)}, bf16[1024,1536]{1,0:T(8,128)(2,1)}, u32[]{:S(2)}) copy-start(bf16[1024,1536]{1,0:T(8,128)(2,1)} %param.8) | copy-start | bytes 9437188
  7.2 120.5 %all-gather.7.cloned.1.call-start = ((), (), s32[]{:S(2)}) async-start(), calls=%async_computation.2 | async-start | bytes 8650752 | tf_op jit(solution)/shard_map/all_gather | solution.py:13
  22.1 3.0 copy-start.5
  24.0 1.1 copy-start.1
  27.3 198.6 %all-gather.5.cloned.1.call-start = ((), (), s32[]{:S(2)}) async-start(), calls=%async_computation.1 | async-start | bytes 8650752 | tf_op jit(solution)/shard_map/all_gather | solution.py:13
  35.4 479.5 %reduce-scatter.4.cloned.1.call-start = ((), (), s32[]{:S(2)}) async-start(), calls=%async_computation.3 | async-start | bytes 6488064 | tf_op jit(solution)/shard_map/reduce_scatter | solution.py:86
  38.0 4.8 copy-start.9
  38.0 4.8 copy-start.6
  42.8 1.9 copy-start.3
  190.6 2.7 copy-start.4
  192.5 0.8 copy-start.8
  258.8 1.9 copy-start.2
  266.1 2.5 copy-start.7
  273.9 5.0 copy-start.10
  514.9 1.7 collective-permute-start
  517.5 7.0 %collective-permute-start.1 = (f32[32,1536]{1,0:T(8,128)S(1)}, f32[32,1536]{1,0:T(8,128)S(1)}, u32[]{:S(2)}, u32[]{:S(2)}) collective-permute-start(f32[32,1536]{1,0:T(8,128)S(1)} %add.132), channel_id=1, source_target_pairs={{0,2},{1,3},{2,0},{3,1},{4,6},{5,7},{6,4},{7,5},{8,10},{9,11},{10,... | collective-permute-start | bytes 589832 | tf_op jit(solution)/shard_map/ppermute | solution.py:94
  524.6 9.6 %collective-permute-start.2 = (f32[32,1536]{1,0:T(8,128)S(1)}, f32[32,1536]{1,0:T(8,128)S(1)}, u32[]{:S(2)}, u32[]{:S(2)}) collective-permute-start(f32[32,1536]{1,0:T(8,128)S(1)} %add.133), channel_id=1, source_target_pairs={{0,4},{1,5},{2,6},{3,7},{4,0},{5,1},{6,2},{7,3},{8,12},{9,13},{10,... | collective-permute-start | bytes 589832 | tf_op jit(solution)/shard_map/ppermute | solution.py:94
Sparse Core Ops, SparseCore 0:
  27.4 100.1 all-gather.6
  130.2 95.6 all-gather.4
  292.9 221.9 reduce-scatter.3
